TPU v7x, 32 devices: a whole 2x2x4 slice. The times are simulated.
32 devices in a mesh: phase: 4 (over y, x), tile: 4 (over z), dp: 2 (over core).
Axes of the slice: x: 2, y: 2, z: 4, core: 2. Of those that a mesh axis runs over, the one named last changes fastest.
Arguments:
- camera_feats: bfloat16 [4, 2, 3, 4, 176, 128], P(None, 'dp', None, 'tile'), may hold values from -6 to 6
- backbone_w: bfloat16 [4, 1152, 128], P('phase'), may hold values from -0.1875 to 0.1875
- depth_w: bfloat16 [128, 118], replicated, may hold values from -1 to 1
- block_tile: int32 [4, 2, 1056, 1], P('phase', 'dp', 'tile'), may hold values from 0 to 3; in each aligned block of 264 rows (0 to 263, 264 to 527, ..., all dimensions but the last counted through in order) at most 264 rows name the same one
- point_slot: int32 [4, 2, 1056, 236], P('phase', 'dp', 'tile'), may hold values from 0 to 15
- block_cells: int32 [4, 2, 1056, 16], P('phase', 'dp', 'tile'), may hold values from 0 to 1024, as said below
- bev_w: bfloat16 [1152, 128], replicated, may hold values from -0.1875 to 0.1875
- cotangent: bfloat16 [4, 2, 16, 256, 128], P('phase', 'dp', 'tile'), may hold values from -6 to 6
Outputs:
- encoded: bfloat16 [4, 2, 16, 256, 128], P('phase', 'dp', 'tile')
- conv_grad: float32 [128, 1152], P('tile')
Inputs may be any that keep to these rules, and one draw needn't show every extreme that they name: `block_tile`: among the 264 blocks of one sample on one index of tile (an aligned run of rows), at most 264 name the same tile. `block_cells`: 1024 marks a slot whose cell lies outside the grid.
All inputs are finite; a program needn't handle non-finite values.
Results may differ from a plain program's by a relative error of at most 0.0085.
Values may be sent and summed in bfloat16 or wider, within the bound.
A program may use at most 64 MiB of HBM per device.

v0:
```python
import jax
import jax.numpy as jnp
from jax import lax
from jax.sharding import PartitionSpec as P

NSEG = 2
BLK = 4
BOUND = 8.0


def extended(cells, sides, width):
    for axis, dim in sides:
        count = lax.axis_size(axis)
        ends = count - 1
        head = lax.slice_in_dim(cells, 0, width, axis=dim)
        tail = lax.slice_in_dim(cells, cells.shape[dim] - width, cells.shape[dim], axis=dim)
        cells = jnp.concatenate(
            [
                lax.ppermute(tail, axis, [(i, (i + 1) % count) for i in range(ends)]),
                cells,
                lax.ppermute(head, axis, [((i + 1) % count, i) for i in range(ends)]),
            ],
            axis=dim,
        )
    return cells


def passed_along(block, axis, distance):
    devices = range(lax.axis_size(axis))
    route = [(i - distance, i) for i in devices if i - distance in devices]
    return lax.ppermute(block, axis, route)


def from_root(block, axis, source):
    block = jnp.where(lax.axis_index(axis) == source, block, jnp.zeros_like(block))
    return lax.psum(block, axis)


def patches_from(padded, row_count, col_count):
    widened = jnp.pad(padded, [(0, 0)] * (padded.ndim - 2) + [(1, 1), (0, 0)])
    shifted = [
        widened[..., row_off : row_off + row_count, col_off : col_off + col_count, :]
        for row_off in range(3)
        for col_off in range(3)
    ]
    stacked = jnp.concatenate(shifted, axis=-1)
    return stacked.reshape(-1, stacked.shape[-1])


def section(images, weight):
    padded = extended(images, (("tile", 2),), 1)
    hidden = jnp.dot(
        patches_from(padded, images.shape[2], images.shape[3]),
        weight,
        preferred_element_type=jnp.float32,
    ).reshape(images.shape)
    return (images.astype(jnp.float32) + jax.nn.silu(hidden)).astype(jnp.bfloat16)


def body(camera_feats, backbone_w, depth_w, block_tile, point_slot, block_cells, bev_w, cotangent):
    phases = lax.axis_size("phase")
    phase_idx = lax.axis_index("phase")
    tile_count = lax.axis_size("tile")
    micro_all = camera_feats.shape[0]
    per_phase = micro_all // phases
    own_weight = backbone_w[0]
    carried = jnp.zeros_like(camera_feats[0])
    collected = jnp.zeros_like(camera_feats)
    steps_total = micro_all + phases - 1
    for step_idx in range(steps_total):
        if step_idx < micro_all:
            entering = jnp.where(phase_idx == 0, camera_feats[step_idx], carried)
        else:
            entering = carried
        leaving = section(entering, own_weight)
        finished = step_idx - (phases - 1)
        if finished >= 0:
            collected = collected.at[finished].set(
                jnp.where(phase_idx == phases - 1, leaving, collected[finished])
            )
        if step_idx + 1 < steps_total:
            carried = passed_along(leaving, "phase", 1)
    everything = from_root(collected, "phase", phases - 1)
    own_feats = lax.dynamic_slice_in_dim(everything, phase_idx * per_phase, per_phase, 0)
    samples_dev = own_feats.shape[0] * own_feats.shape[1]
    channels = own_feats.shape[-1]
    context = own_feats.reshape(samples_dev, -1, channels)
    positions = context.shape[1]
    seg_len = depth_w.shape[1] // NSEG
    slot_total = block_cells.shape[-1]
    pos_groups = positions // BLK
    block_count = pos_groups * NSEG
    logits = jnp.dot(context.reshape(-1, channels), depth_w, preferred_element_type=jnp.float32)
    depth_prob = jax.nn.softmax(BOUND * jnp.tanh(logits / BOUND), axis=-1)
    depth_blocks = (
        depth_prob.reshape(samples_dev, pos_groups, BLK, NSEG, seg_len)
        .transpose(0, 1, 3, 2, 4)
        .reshape(samples_dev, block_count, BLK, seg_len)
    )
    slot_blocks = point_slot.reshape(samples_dev, block_count, BLK, seg_len)
    splat_w = jnp.stack(
        [
            jnp.sum(
                jnp.where(slot_blocks == target, depth_blocks, jnp.zeros_like(depth_blocks)),
                axis=-1,
            )
            for target in range(slot_total)
        ],
        axis=2,
    ).astype(jnp.bfloat16)
    block_ctx = jnp.repeat(context.reshape(samples_dev, pos_groups, BLK, channels), NSEG, axis=1)
    row_count = cotangent.shape[2]
    col_count = cotangent.shape[3]
    cells_tile = row_count * col_count
    capacity = max(2, 4 * block_count // tile_count)
    targets = block_tile.reshape(samples_dev, block_count)
    member = (targets[..., None] == jnp.arange(tile_count, dtype=jnp.int32)).astype(jnp.int32)
    slot_rank = jnp.sum((jnp.cumsum(member, axis=1) - 1) * member, axis=-1)
    slot_flat = targets * capacity + slot_rank
    sample_rows = jnp.broadcast_to(
        jnp.arange(samples_dev, dtype=jnp.int32)[:, None], slot_flat.shape
    )
    send_ctx = (
        jnp.zeros((samples_dev, tile_count * capacity, BLK, channels), jnp.bfloat16)
        .at[sample_rows, slot_flat]
        .set(block_ctx)
    )
    send_weights = (
        jnp.zeros((samples_dev, tile_count * capacity, slot_total, BLK), jnp.bfloat16)
        .at[sample_rows, slot_flat]
        .set(splat_w)
    )
    send_cells = (
        jnp.full((samples_dev, tile_count * capacity, slot_total), cells_tile, jnp.int32)
        .at[sample_rows, slot_flat]
        .set(block_cells.reshape(samples_dev, block_count, slot_total))
    )
    send_ctx = send_ctx.reshape(samples_dev, tile_count, capacity, BLK, channels)
    send_weights = send_weights.reshape(samples_dev, tile_count, capacity, slot_total, BLK)
    send_cells = send_cells.reshape(samples_dev, tile_count, capacity, slot_total)
    got_ctx, got_weights, got_cells = (
        lax.all_to_all(send_ctx, "tile", split_axis=1, concat_axis=1, tiled=True),
        lax.all_to_all(send_weights, "tile", split_axis=1, concat_axis=1, tiled=True),
        lax.all_to_all(send_cells, "tile", split_axis=1, concat_axis=1, tiled=True),
    )
    pooled = jnp.einsum(
        "ankti,ankic->anktc", got_weights, got_ctx, preferred_element_type=jnp.float32
    ).astype(jnp.bfloat16)
    group_size = min(8, tile_count)
    group_count = tile_count // group_size
    group_rows = group_size * capacity * slot_total
    pooled_groups = jnp.moveaxis(
        pooled.reshape(samples_dev, group_count, group_rows, channels), 1, 0
    )
    cell_groups = jnp.moveaxis(got_cells.reshape(samples_dev, group_count, group_rows), 1, 0)
    cell_range = jnp.arange(cells_tile, dtype=jnp.int32).reshape(1, cells_tile, 1)

    def splat_group(grid_sum, pieces):
        part_pooled, part_cells = pieces
        one_hot = (part_cells[:, None, :] == cell_range).astype(jnp.bfloat16)
        grid_sum = grid_sum + jnp.einsum(
            "sxr,src->sxc", one_hot, part_pooled, preferred_element_type=jnp.float32
        )
        return (grid_sum, None)

    totals, _ = lax.scan(
        splat_group,
        jnp.zeros((samples_dev, cells_tile, channels), jnp.float32),
        (pooled_groups, cell_groups),
    )
    bev_grid = totals.astype(jnp.bfloat16).reshape(samples_dev, row_count, col_count, channels)
    padded_grid = extended(bev_grid, (("tile", 1),), 1)
    bev_patches = patches_from(padded_grid, row_count, col_count)
    mixed = jnp.dot(bev_patches, bev_w, preferred_element_type=jnp.float32)
    encoded = (
        (bev_grid.astype(jnp.float32).reshape(-1, channels) + mixed)
        .astype(jnp.bfloat16)
        .reshape(cotangent.shape)
    )
    upstream = cotangent.reshape(-1, channels)
    total_cells = (
        micro_all * cotangent.shape[1] * lax.axis_size("dp") * row_count * tile_count * col_count
    )
    grad_scale = float(total_cells) ** (-0.5)
    grad_share = lax.psum_scatter(
        grad_scale
        * lax.dot_general(
            upstream, bev_patches, (((0,), (0,)), ((), ())), preferred_element_type=jnp.float32
        ),
        "tile",
        scatter_dimension=0,
        tiled=True,
    )
    conv_grad = lax.psum(grad_share, ("phase", "dp"))
    return (encoded, conv_grad)


def solution(mesh):
    return jax.shard_map(
        body,
        mesh=mesh,
        in_specs=(
            P(None, "dp", None, "tile", None, None),
            P("phase", None, None),
            P(),
            P("phase", "dp", "tile", None),
            P("phase", "dp", "tile", None),
            P("phase", "dp", "tile", None),
            P(),
            P("phase", "dp", "tile", None, None),
        ),
        out_specs=(P("phase", "dp", "tile", None, None), P("tile", None)),
        check_vma=False,
    )
```

profile of v0, /device:TPU:0, one launch (start us, length us, event | category | flops | bytes accessed | tf_op | source)
XLA Modules:
  0.0 385.2 jit_solution(11881665665288128379)
XLA Ops:
  8.2 4.9 %collective-permute-start = (bf16[1,3,1,176,128]{4,3,1,2,0:T(8,128)(2,1)S(1)}, bf16[1,3,1,176,128]{4,3,1,2,0:T(8,128)(2,1)S(1)}, u32[]{:S(2)}, u32[]{:S(2)}) collective-permute-start(bf16[1,3,1,176,128]{4,3,1,2,0:T(8,128)(2,1)S(1)} %fusion.83), channel_id=1, source_target_pairs={{0,2},{2,4},{4,6},{1,3},{3,5},{5,7},{8,10},{10,12},{12,14},{9,11},... | collective-permute-start | bytes 405512 | tf_op jit(solution)/shard_map/ppermute | solution.py:19
  15.9 4.1 %collective-permute-done.1 = bf16[1,3,1,176,128]{4,3,1,2,0:T(8,128)(2,1)S(1)} collective-permute-done((bf16[1,3,1,176,128]{4,3,1,2,0:T(8,128)(2,1)S(1)}, bf16[1,3,1,176,128]{4,3,1,2,0:T(8,128)(2,1)S(1)}, u32[]{:S(2)}, u32[]{:S(2)}) %collective-permute-start.1) | collective-permute-done | bytes 135200 | tf_op jit(solution)/shard_map/ppermute | solution.py:21
  21.8 3.4 collective-permute-start.2
  25.2 2.5 collective-permute-done.2
  27.8 3.5 collective-permute-start.3
  33.8 4.4 %collective-permute-done.4 = bf16[1,3,1,176,128]{4,3,1,2,0:T(8,128)(2,1)S(1)} collective-permute-done((bf16[1,3,1,176,128]{4,3,1,2,0:T(8,128)(2,1)S(1)}, bf16[1,3,1,176,128]{4,3,1,2,0:T(8,128)(2,1)S(1)}, u32[]{:S(2)}, u32[]{:S(2)}) %collective-permute-start.4) | collective-permute-done | bytes 135200 | tf_op jit(solution)/shard_map/ppermute | solution.py:21
  39.3 4.4 %collective-permute-start.5 = (bf16[1,3,1,176,128]{4,3,1,2,0:T(8,128)(2,1)S(1)}, bf16[1,3,1,176,128]{4,3,1,2,0:T(8,128)(2,1)S(1)}, u32[]{:S(2)}, u32[]{:S(2)}) collective-permute-start(bf16[1,3,1,176,128]{4,3,1,2,0:T(8,128)(2,1)S(1)} %add_convert_fusion.5), channel_id=1, source_target_pairs={{0,8},{8,16},{16,24},{1,9},{9,17},{17,25},{2,10},{10,18},{18,26},{... | collective-permute-start | bytes 405512 | tf_op jit(solution)/shard_map/ppermute | solution.py:31
  46.3 3.5 collective-permute-start.6
  52.3 4.4 %collective-permute-done.7 = bf16[1,3,1,176,128]{4,3,1,2,0:T(8,128)(2,1)S(1)} collective-permute-done((bf16[1,3,1,176,128]{4,3,1,2,0:T(8,128)(2,1)S(1)}, bf16[1,3,1,176,128]{4,3,1,2,0:T(8,128)(2,1)S(1)}, u32[]{:S(2)}, u32[]{:S(2)}) %collective-permute-start.7) | collective-permute-done | bytes 135200 | tf_op jit(solution)/shard_map/ppermute | solution.py:21
  57.8 4.4 %collective-permute-start.8 = (bf16[1,3,1,176,128]{4,3,1,2,0:T(8,128)(2,1)S(1)}, bf16[1,3,1,176,128]{4,3,1,2,0:T(8,128)(2,1)S(1)}, u32[]{:S(2)}, u32[]{:S(2)}) collective-permute-start(bf16[1,3,1,176,128]{4,3,1,2,0:T(8,128)(2,1)S(1)} %add_convert_fusion.4), channel_id=1, source_target_pairs={{0,8},{8,16},{16,24},{1,9},{9,17},{17,25},{2,10},{10,18},{18,26},{... | collective-permute-start | bytes 405512 | tf_op jit(solution)/shard_map/ppermute | solution.py:31
  62.2 2.5 collective-permute-done.8
  66.1 4.6 %collective-permute-start.9 = (bf16[1,3,1,176,128]{4,3,1,2,0:T(8,128)(2,1)S(1)}, bf16[1,3,1,176,128]{4,3,1,2,0:T(8,128)(2,1)S(1)}, u32[]{:S(2)}, u32[]{:S(2)}) collective-permute-start(bf16[1,3,1,176,128]{4,3,1,2,0:T(8,128)(2,1)S(1)} %fusion.57), channel_id=1, source_target_pairs={{0,2},{2,4},{4,6},{1,3},{3,5},{5,7},{8,10},{10,12},{12,14},{9,11},... | collective-permute-start | bytes 405512 | tf_op jit(solution)/shard_map/ppermute | solution.py:19
  74.4 5.2 %collective-permute-start.11 = (bf16[1,3,1,176,128]{4,3,1,2,0:T(8,128)(2,1)S(1)}, bf16[1,3,1,176,128]{4,3,1,2,0:T(8,128)(2,1)S(1)}, u32[]{:S(2)}, u32[]{:S(2)}) collective-permute-start(bf16[1,3,1,176,128]{4,3,1,2,0:T(8,128)(2,1)S(1)} %get-tuple-element.92), channel_id=1, source_target_pairs={{0,8},{8,16},{16,24},{1,9},{9,17},{17,25},{2,10},{10,18},{18,26},{... | collective-permute-start | bytes 405512 | tf_op jit(solution)/shard_map/ppermute | solution.py:31
  79.6 2.5 collective-permute-done.11
  82.1 4.4 %collective-permute-start.12 = (bf16[1,3,1,176,128]{4,3,1,2,0:T(8,128)(2,1)S(1)}, bf16[1,3,1,176,128]{4,3,1,2,0:T(8,128)(2,1)S(1)}, u32[]{:S(2)}, u32[]{:S(2)}) collective-permute-start(bf16[1,3,1,176,128]{4,3,1,2,0:T(8,128)(2,1)S(1)} %collective-permute-done.11), channel_id=1, source_target_pairs={{0,2},{2,4},{4,6},{1,3},{3,5},{5,7},{8,10},{10,12},{12,14},{9,11},... | collective-permute-start | bytes 405512 | tf_op jit(solution)/shard_map/ppermute | solution.py:19
  89.0 4.4 %collective-permute-done.13 = bf16[1,3,1,176,128]{4,3,1,2,0:T(8,128)(2,1)S(1)} collective-permute-done((bf16[1,3,1,176,128]{4,3,1,2,0:T(8,128)(2,1)S(1)}, bf16[1,3,1,176,128]{4,3,1,2,0:T(8,128)(2,1)S(1)}, u32[]{:S(2)}, u32[]{:S(2)}) %collective-permute-start.13) | collective-permute-done | bytes 135200 | tf_op jit(solution)/shard_map/ppermute | solution.py:21
  94.6 5.3 %collective-permute-start.14 = (bf16[1,3,1,176,128]{4,3,1,2,0:T(8,128)(2,1)S(1)}, bf16[1,3,1,176,128]{4,3,1,2,0:T(8,128)(2,1)S(1)}, u32[]{:S(2)}, u32[]{:S(2)}) collective-permute-start(bf16[1,3,1,176,128]{4,3,1,2,0:T(8,128)(2,1)S(1)} %get-tuple-element.90), channel_id=1, source_target_pairs={{0,8},{8,16},{16,24},{1,9},{9,17},{17,25},{2,10},{10,18},{18,26},{... | collective-permute-start | bytes 405512 | tf_op jit(solution)/shard_map/ppermute | solution.py:31
  107.1 4.1 %collective-permute-done.16 = bf16[1,3,1,176,128]{4,3,1,2,0:T(8,128)(2,1)S(1)} collective-permute-done((bf16[1,3,1,176,128]{4,3,1,2,0:T(8,128)(2,1)S(1)}, bf16[1,3,1,176,128]{4,3,1,2,0:T(8,128)(2,1)S(1)}, u32[]{:S(2)}, u32[]{:S(2)}) %collective-permute-start.16) | collective-permute-done | bytes 135200 | tf_op jit(solution)/shard_map/ppermute | solution.py:21
  112.4 5.3 %collective-permute-start.17 = (bf16[1,3,1,176,128]{4,3,1,2,0:T(8,128)(2,1)S(1)}, bf16[1,3,1,176,128]{4,3,1,2,0:T(8,128)(2,1)S(1)}, u32[]{:S(2)}, u32[]{:S(2)}) collective-permute-start(bf16[1,3,1,176,128]{4,3,1,2,0:T(8,128)(2,1)S(1)} %get-tuple-element.88), channel_id=1, source_target_pairs={{0,8},{8,16},{16,24},{1,9},{9,17},{17,25},{2,10},{10,18},{18,26},{... | collective-permute-start | bytes 405512 | tf_op jit(solution)/shard_map/ppermute | solution.py:31
  124.7 4.4 %collective-permute-done.19 = bf16[1,3,1,176,128]{4,3,1,2,0:T(8,128)(2,1)S(1)} collective-permute-done((bf16[1,3,1,176,128]{4,3,1,2,0:T(8,128)(2,1)S(1)}, bf16[1,3,1,176,128]{4,3,1,2,0:T(8,128)(2,1)S(1)}, u32[]{:S(2)}, u32[]{:S(2)}) %collective-permute-start.19) | collective-permute-done | bytes 135200 | tf_op jit(solution)/shard_map/ppermute | solution.py:21
  133.5 3.5 all-to-all-start
  141.2 36.8 %all-reduce.14.cloned.1.call-done = bf16[4,1,3,1,176,128]{5,4,2,3,1,0:T(8,128)(2,1)} async-done(((bf16[4,1,3,1,176,128]{5,4,2,3,1,0:T(8,128)(2,1)}), bf16[4,1,3,1,176,128]{5,4,2,3,1,0:T(8,128)(2,1)}) %all-reduce.14.cloned.1.call-update) | async-done | bytes 540688 | tf_op jit(solution)/shard_map/psum | solution.py:36
  180.1 7.7 %fusion.26 = (bf16[132,2,4]{2,1,0:T(2,128)(2,1)S(1)}, bf16[132,2,4]{2,1,0:T(2,128)(2,1)S(1)}, bf16[132,2,4]{2,1,0:T(2,128)(2,1)S(1)}, bf16[132,2,4]{2,1,0:T(2,12...) fusion(pred[1,132,2,4,59]{4,3,2,1,0:T(4,128)(4,1)S(1)} %eq.411,, ...), kind=kLoop, calls=%fused_computation.54 | loop fusion | flops 1976832 | bytes 1279872 | tf_op jit(solution)/shard_map/reduce_sum | solution.py:103
  202.1 8.6 %scatter_fusion = bf16[1056,16,4]{1,2,0:T(4,128)(2,1)S(1)} fusion(bf16[1056,16,4]{1,2,0:T(4,128)(2,1)S(1)} %broadcast.618, s32[264]{0:T(512)S(1)} %fusion.62, bf16[264,16,4]{1,2,0:T(4,128)(2,1)S(1)} %copy.70), kind=kCustom, calls=%fused_computation.1 | custom fusion | bytes 102432 | tf_op jit(solution)/shard_map/scatter | solution.py:131
  212.0 4.6 %all-to-all-start.1 = ((bf16[1,4,264,16,4]{2,3,4,0,1:T(8,128)(2,1)}), bf16[1,4,264,16,4]{2,3,4,0,1:T(8,128)(2,1)S(1)}, u32[]{:S(2)}, u32[]{:S(2)}) async-start(bf16[1,4,264,16,4]{2,3,4,0,1:T(8,128)(2,1)} %copy.71), calls=%async_computation.1 | async-start | bytes 393216 | tf_op jit(solution)/shard_map/all_to_all | solution.py:143
  217.8 26.7 %scatter_fusion.1 = bf16[1056,4,128]{2,1,0:T(4,128)(2,1)} fusion(bf16[1056,4,128]{2,1,0:T(4,128)(2,1)} %broadcast.620, s32[264]{0:T(512)S(1)} %fusion.62, bf16[264,4,128]{2,1,0:T(4,128)(2,1)S(1)} %bitcast.272), kind=kCustom, calls=%fused_computation.2 | custom fusion | bytes 812064 | tf_op jit(solution)/shard_map/scatter | solution.py:126
  244.6 5.1 %all-to-all-start.2 = ((bf16[1,4,264,4,128]{4,3,2,0,1:T(4,128)(2,1)}), bf16[1,4,264,4,128]{4,3,2,0,1:T(4,128)(2,1)S(1)}, u32[]{:S(2)}, u32[]{:S(2)}) async-start(bf16[1,4,264,4,128]{4,3,2,0,1:T(4,128)(2,1)} %bitcast.70), calls=%async_computation.2 | async-start | bytes 2162688 | tf_op jit(solution)/shard_map/all_to_all | solution.py:142
  250.8 24.5 %all-to-all-done.2 = bf16[1,4,264,4,128]{4,3,2,0,1:T(4,128)(2,1)S(1)} async-done(((bf16[1,4,264,4,128]{4,3,2,0,1:T(4,128)(2,1)}), bf16[1,4,264,4,128]{4,3,2,0,1:T(4,128)(2,1)S(1)}, u32[]{:S(2)}, u32[]{:S(2)}) %all-to-all-start.2) | async-done | bytes 1081376 | tf_op jit(solution)/shard_map/all_to_all | solution.py:142
  277.0 10.5 %fusion.4 = bf16[1024,128]{1,0:T(8,128)(2,1)S(1)} fusion(bf16[16896,128]{1,0:T(8,128)(2,1)S(1)} %bitcast.247, s32[16896]{0:T(1024)S(1)} %eq.358), kind=kOutput, calls=%fused_computation.15 | convolution fusion | flops 4446617600 | bytes 4655104 | tf_op jit(solution)/shard_map/while/body/eval_jaxpr/sxr,src->sxc/dot_general | solution.py:161
  290.8 4.3 %collective-permute-done.21 = bf16[1,1,256,128]{3,2,1,0:T(8,128)(2,1)S(1)} collective-permute-done((bf16[1,1,256,128]{3,2,1,0:T(8,128)(2,1)S(1)}, bf16[1,1,256,128]{3,2,1,0:T(8,128)(2,1)S(1)}, u32[]{:S(2)}, u32[]{:S(2)}) %collective-permute-start.21) | collective-permute-done | bytes 65568 | tf_op jit(solution)/shard_map/ppermute | solution.py:21
  298.7 21.6 %reduce-scatter.4.cloned.1.call-done = f32[32,1152]{1,0:T(8,128)} async-done(((f32[128,1152]{1,0:T(8,128)}), f32[32,1152]{1,0:T(8,128)}) %reduce-scatter.4.cloned.1.call-update) | async-done | bytes 147472
  323.7 53.0 %all-reduce.16.cloned.1.call-done = f32[32,1152]{0,1:T(8,128)} async-done(((f32[32,1152]{0,1:T(8,128)}), f32[32,1152]{0,1:T(8,128)}) %all-reduce.16.cloned.1.call-update) | async-done | bytes 147472 | tf_op jit(solution)/shard_map/psum | solution.py:194
  (224 shorter events, 81.3 us)
Async XLA Ops:
  7.2 13.6 %copy-start = (bf16[1,1152,128]{2,1,0:T(8,128)(2,1)S(1)}, bf16[1,1152,128]{2,1,0:T(8,128)(2,1)}, u32[]{:S(2)}) copy-start(bf16[1,1152,128]{2,1,0:T(8,128)(2,1)} %param.17) | copy-start | bytes 884740
  7.2 170.8 %all-reduce.14.cloned.1.call-start = ((), (), s32[]{:S(2)}) async-start(), calls=%async_computation.4 | async-start | bytes 1081344 | tf_op jit(solution)/shard_map/psum | solution.py:36
  8.2 7.8 %collective-permute-start = (bf16[1,3,1,176,128]{4,3,1,2,0:T(8,128)(2,1)S(1)}, bf16[1,3,1,176,128]{4,3,1,2,0:T(8,128)(2,1)S(1)}, u32[]{:S(2)}, u32[]{:S(2)}) collective-permute-start(bf16[1,3,1,176,128]{4,3,1,2,0:T(8,128)(2,1)S(1)} %fusion.83), channel_id=1, source_target_pairs={{0,2},{2,4},{4,6},{1,3},{3,5},{5,7},{8,10},{10,12},{12,14},{9,11},... | collective-permute-start | bytes 405512 | tf_op jit(solution)/shard_map/ppermute | solution.py:19
  13.1 6.9 %collective-permute-start.1 = (bf16[1,3,1,176,128]{4,3,1,2,0:T(8,128)(2,1)S(1)}, bf16[1,3,1,176,128]{4,3,1,2,0:T(8,128)(2,1)S(1)}, u32[]{:S(2)}, u32[]{:S(2)}) collective-permute-start(bf16[1,3,1,176,128]{4,3,1,2,0:T(8,128)(2,1)S(1)} %fusion.83), channel_id=1, source_target_pairs={{2,0},{4,2},{6,4},{3,1},{5,3},{7,5},{10,8},{12,10},{14,12},{11,9},... | collective-permute-start | bytes 405512 | tf_op jit(solution)/shard_map/ppermute | solution.py:21
  21.8 5.9 %collective-permute-start.2 = (bf16[1,3,1,176,128]{4,3,1,2,0:T(8,128)(2,1)S(1)}, bf16[1,3,1,176,128]{4,3,1,2,0:T(8,128)(2,1)S(1)}, u32[]{:S(2)}, u32[]{:S(2)}) collective-permute-start(bf16[1,3,1,176,128]{4,3,1,2,0:T(8,128)(2,1)S(1)} %add_convert_fusion.6), channel_id=1, source_target_pairs={{0,8},{8,16},{16,24},{1,9},{9,17},{17,25},{2,10},{10,18},{18,26},{... | collective-permute-start | bytes 405512 | tf_op jit(solution)/shard_map/ppermute | solution.py:31
  27.8 6.0 %collective-permute-start.3 = (bf16[1,3,1,176,128]{4,3,1,2,0:T(8,128)(2,1)S(1)}, bf16[1,3,1,176,128]{4,3,1,2,0:T(8,128)(2,1)S(1)}, u32[]{:S(2)}, u32[]{:S(2)}) collective-permute-start(bf16[1,3,1,176,128]{4,3,1,2,0:T(8,128)(2,1)S(1)} %fusion.56), channel_id=1, source_target_pairs={{0,2},{2,4},{4,6},{1,3},{3,5},{5,7},{8,10},{10,12},{12,14},{9,11},... | collective-permute-start | bytes 405512 | tf_op jit(solution)/shard_map/ppermute | solution.py:19
  31.3 6.9 %collective-permute-start.4 = (bf16[1,3,1,176,128]{4,3,1,2,0:T(8,128)(2,1)S(1)}, bf16[1,3,1,176,128]{4,3,1,2,0:T(8,128)(2,1)S(1)}, u32[]{:S(2)}, u32[]{:S(2)}) collective-permute-start(bf16[1,3,1,176,128]{4,3,1,2,0:T(8,128)(2,1)S(1)} %fusion.56), channel_id=1, source_target_pairs={{2,0},{4,2},{6,4},{3,1},{5,3},{7,5},{10,8},{12,10},{14,12},{11,9},... | collective-permute-start | bytes 405512 | tf_op jit(solution)/shard_map/ppermute | solution.py:21
  39.3 6.9 %collective-permute-start.5 = (bf16[1,3,1,176,128]{4,3,1,2,0:T(8,128)(2,1)S(1)}, bf16[1,3,1,176,128]{4,3,1,2,0:T(8,128)(2,1)S(1)}, u32[]{:S(2)}, u32[]{:S(2)}) collective-permute-start(bf16[1,3,1,176,128]{4,3,1,2,0:T(8,128)(2,1)S(1)} %add_convert_fusion.5), channel_id=1, source_target_pairs={{0,8},{8,16},{16,24},{1,9},{9,17},{17,25},{2,10},{10,18},{18,26},{... | collective-permute-start | bytes 405512 | tf_op jit(solution)/shard_map/ppermute | solution.py:31
  46.3 6.0 %collective-permute-start.6 = (bf16[1,3,1,176,128]{4,3,1,2,0:T(8,128)(2,1)S(1)}, bf16[1,3,1,176,128]{4,3,1,2,0:T(8,128)(2,1)S(1)}, u32[]{:S(2)}, u32[]{:S(2)}) collective-permute-start(bf16[1,3,1,176,128]{4,3,1,2,0:T(8,128)(2,1)S(1)} %bitcast_select_fusion.16), channel_id=1, source_target_pairs={{0,2},{2,4},{4,6},{1,3},{3,5},{5,7},{8,10},{10,12},{12,14},{9,11},... | collective-permute-start | bytes 405512 | tf_op jit(solution)/shard_map/ppermute | solution.py:19
  49.8 6.9 %collective-permute-start.7 = (bf16[1,3,1,176,128]{4,3,1,2,0:T(8,128)(2,1)S(1)}, bf16[1,3,1,176,128]{4,3,1,2,0:T(8,128)(2,1)S(1)}, u32[]{:S(2)}, u32[]{:S(2)}) collective-permute-start(bf16[1,3,1,176,128]{4,3,1,2,0:T(8,128)(2,1)S(1)} %bitcast_select_fusion.16), channel_id=1, source_target_pairs={{2,0},{4,2},{6,4},{3,1},{5,3},{7,5},{10,8},{12,10},{14,12},{11,9},... | collective-permute-start | bytes 405512 | tf_op jit(solution)/shard_map/ppermute | solution.py:21
  57.8 6.9 %collective-permute-start.8 = (bf16[1,3,1,176,128]{4,3,1,2,0:T(8,128)(2,1)S(1)}, bf16[1,3,1,176,128]{4,3,1,2,0:T(8,128)(2,1)S(1)}, u32[]{:S(2)}, u32[]{:S(2)}) collective-permute-start(bf16[1,3,1,176,128]{4,3,1,2,0:T(8,128)(2,1)S(1)} %add_convert_fusion.4), channel_id=1, source_target_pairs={{0,8},{8,16},{16,24},{1,9},{9,17},{17,25},{2,10},{10,18},{18,26},{... | collective-permute-start | bytes 405512 | tf_op jit(solution)/shard_map/ppermute | solution.py:31
  64.8 6.9 %collective-permute-start.10 = (bf16[1,3,1,176,128]{4,3,1,2,0:T(8,128)(2,1)S(1)}, bf16[1,3,1,176,128]{4,3,1,2,0:T(8,128)(2,1)S(1)}, u32[]{:S(2)}, u32[]{:S(2)}) collective-permute-start(bf16[1,3,1,176,128]{4,3,1,2,0:T(8,128)(2,1)S(1)} %fusion.57), channel_id=1, source_target_pairs={{2,0},{4,2},{6,4},{3,1},{5,3},{7,5},{10,8},{12,10},{14,12},{11,9},... | collective-permute-start | bytes 405512 | tf_op jit(solution)/shard_map/ppermute | solution.py:21
  66.1 7.1 %collective-permute-start.9 = (bf16[1,3,1,176,128]{4,3,1,2,0:T(8,128)(2,1)S(1)}, bf16[1,3,1,176,128]{4,3,1,2,0:T(8,128)(2,1)S(1)}, u32[]{:S(2)}, u32[]{:S(2)}) collective-permute-start(bf16[1,3,1,176,128]{4,3,1,2,0:T(8,128)(2,1)S(1)} %fusion.57), channel_id=1, source_target_pairs={{0,2},{2,4},{4,6},{1,3},{3,5},{5,7},{8,10},{10,12},{12,14},{9,11},... | collective-permute-start | bytes 405512 | tf_op jit(solution)/shard_map/ppermute | solution.py:19
  74.4 7.7 %collective-permute-start.11 = (bf16[1,3,1,176,128]{4,3,1,2,0:T(8,128)(2,1)S(1)}, bf16[1,3,1,176,128]{4,3,1,2,0:T(8,128)(2,1)S(1)}, u32[]{:S(2)}, u32[]{:S(2)}) collective-permute-start(bf16[1,3,1,176,128]{4,3,1,2,0:T(8,128)(2,1)S(1)} %get-tuple-element.92), channel_id=1, source_target_pairs={{0,8},{8,16},{16,24},{1,9},{9,17},{17,25},{2,10},{10,18},{18,26},{... | collective-permute-start | bytes 405512 | tf_op jit(solution)/shard_map/ppermute | solution.py:31
  82.1 6.9 %collective-permute-start.12 = (bf16[1,3,1,176,128]{4,3,1,2,0:T(8,128)(2,1)S(1)}, bf16[1,3,1,176,128]{4,3,1,2,0:T(8,128)(2,1)S(1)}, u32[]{:S(2)}, u32[]{:S(2)}) collective-permute-start(bf16[1,3,1,176,128]{4,3,1,2,0:T(8,128)(2,1)S(1)} %collective-permute-done.11), channel_id=1, source_target_pairs={{0,2},{2,4},{4,6},{1,3},{3,5},{5,7},{8,10},{10,12},{12,14},{9,11},... | collective-permute-start | bytes 405512 | tf_op jit(solution)/shard_map/ppermute | solution.py:19
  86.5 6.9 %collective-permute-start.13 = (bf16[1,3,1,176,128]{4,3,1,2,0:T(8,128)(2,1)S(1)}, bf16[1,3,1,176,128]{4,3,1,2,0:T(8,128)(2,1)S(1)}, u32[]{:S(2)}, u32[]{:S(2)}) collective-permute-start(bf16[1,3,1,176,128]{4,3,1,2,0:T(8,128)(2,1)S(1)} %collective-permute-done.11), channel_id=1, source_target_pairs={{2,0},{4,2},{6,4},{3,1},{5,3},{7,5},{10,8},{12,10},{14,12},{11,9},... | collective-permute-start | bytes 405512 | tf_op jit(solution)/shard_map/ppermute | solution.py:21
  93.9 5.9 %copy-start.6 = (s32[1,1,264,1]{2,3,1,0:T(1,128)S(1)}, s32[1,1,264,1]{2,3,1,0:T(1,128)}, u32[]{:S(2)}) copy-start(s32[1,1,264,1]{2,3,1,0:T(1,128)} %param.19) | copy-start | bytes 3172
  94.6 7.8 %collective-permute-start.14 = (bf16[1,3,1,176,128]{4,3,1,2,0:T(8,128)(2,1)S(1)}, bf16[1,3,1,176,128]{4,3,1,2,0:T(8,128)(2,1)S(1)}, u32[]{:S(2)}, u32[]{:S(2)}) collective-permute-start(bf16[1,3,1,176,128]{4,3,1,2,0:T(8,128)(2,1)S(1)} %get-tuple-element.90), channel_id=1, source_target_pairs={{0,8},{8,16},{16,24},{1,9},{9,17},{17,25},{2,10},{10,18},{18,26},{... | collective-permute-start | bytes 405512 | tf_op jit(solution)/shard_map/ppermute | solution.py:31
  102.4 4.7 %collective-permute-start.15 = (bf16[1,3,1,176,128]{4,3,1,2,0:T(8,128)(2,1)S(1)}, bf16[1,3,1,176,128]{4,3,1,2,0:T(8,128)(2,1)S(1)}, u32[]{:S(2)}, u32[]{:S(2)}) collective-permute-start(bf16[1,3,1,176,128]{4,3,1,2,0:T(8,128)(2,1)S(1)} %collective-permute-done.14), channel_id=1, source_target_pairs={{0,2},{2,4},{4,6},{1,3},{3,5},{5,7},{8,10},{10,12},{12,14},{9,11},... | collective-permute-start | bytes 405512 | tf_op jit(solution)/shard_map/ppermute | solution.py:19
  104.3 6.9 %collective-permute-start.16 = (bf16[1,3,1,176,128]{4,3,1,2,0:T(8,128)(2,1)S(1)}, bf16[1,3,1,176,128]{4,3,1,2,0:T(8,128)(2,1)S(1)}, u32[]{:S(2)}, u32[]{:S(2)}) collective-permute-start(bf16[1,3,1,176,128]{4,3,1,2,0:T(8,128)(2,1)S(1)} %collective-permute-done.14), channel_id=1, source_target_pairs={{2,0},{4,2},{6,4},{3,1},{5,3},{7,5},{10,8},{12,10},{14,12},{11,9},... | collective-permute-start | bytes 405512 | tf_op jit(solution)/shard_map/ppermute | solution.py:21
  112.4 7.8 %collective-permute-start.17 = (bf16[1,3,1,176,128]{4,3,1,2,0:T(8,128)(2,1)S(1)}, bf16[1,3,1,176,128]{4,3,1,2,0:T(8,128)(2,1)S(1)}, u32[]{:S(2)}, u32[]{:S(2)}) collective-permute-start(bf16[1,3,1,176,128]{4,3,1,2,0:T(8,128)(2,1)S(1)} %get-tuple-element.88), channel_id=1, source_target_pairs={{0,8},{8,16},{16,24},{1,9},{9,17},{17,25},{2,10},{10,18},{18,26},{... | collective-permute-start | bytes 405512 | tf_op jit(solution)/shard_map/ppermute | solution.py:31
  120.2 4.4 %collective-permute-start.18 = (bf16[1,3,1,176,128]{4,3,1,2,0:T(8,128)(2,1)S(1)}, bf16[1,3,1,176,128]{4,3,1,2,0:T(8,128)(2,1)S(1)}, u32[]{:S(2)}, u32[]{:S(2)}) collective-permute-start(bf16[1,3,1,176,128]{4,3,1,2,0:T(8,128)(2,1)S(1)} %collective-permute-done.17), channel_id=1, source_target_pairs={{0,2},{2,4},{4,6},{1,3},{3,5},{5,7},{8,10},{10,12},{12,14},{9,11},... | collective-permute-start | bytes 405512 | tf_op jit(solution)/shard_map/ppermute | solution.py:19
  122.2 6.9 %collective-permute-start.19 = (bf16[1,3,1,176,128]{4,3,1,2,0:T(8,128)(2,1)S(1)}, bf16[1,3,1,176,128]{4,3,1,2,0:T(8,128)(2,1)S(1)}, u32[]{:S(2)}, u32[]{:S(2)}) collective-permute-start(bf16[1,3,1,176,128]{4,3,1,2,0:T(8,128)(2,1)S(1)} %collective-permute-done.17), channel_id=1, source_target_pairs={{2,0},{4,2},{6,4},{3,1},{5,3},{7,5},{10,8},{12,10},{14,12},{11,9},... | collective-permute-start | bytes 405512 | tf_op jit(solution)/shard_map/ppermute | solution.py:21
  133.5 78.5 %all-to-all-start = ((s32[1,4,264,16]{2,3,0,1:T(8,128)}), s32[1,4,264,16]{2,3,0,1:T(8,128)S(1)}, u32[]{:S(2)}, u32[]{:S(2)}) async-start(s32[1,4,264,16]{2,3,0,1:T(8,128)} %copy.48), calls=%async_computation | async-start | bytes 196608 | tf_op jit(solution)/shard_map/all_to_all | solution.py:144
  138.7 40.2 %copy-start.4 = (bf16[128,118]{0,1:T(8,128)(2,1)S(1)}, bf16[128,118]{0,1:T(8,128)(2,1)}, u32[]{:S(2)}) copy-start(bf16[128,118]{0,1:T(8,128)(2,1)} %param.18) | copy-start | bytes 90628
  212.0 32.5 %all-to-all-start.1 = ((bf16[1,4,264,16,4]{2,3,4,0,1:T(8,128)(2,1)}), bf16[1,4,264,16,4]{2,3,4,0,1:T(8,128)(2,1)S(1)}, u32[]{:S(2)}, u32[]{:S(2)}) async-start(bf16[1,4,264,16,4]{2,3,4,0,1:T(8,128)(2,1)} %copy.71), calls=%async_computation.1 | async-start | bytes 393216 | tf_op jit(solution)/shard_map/all_to_all | solution.py:143
  244.6 30.7 %all-to-all-start.2 = ((bf16[1,4,264,4,128]{4,3,2,0,1:T(4,128)(2,1)}), bf16[1,4,264,4,128]{4,3,2,0,1:T(4,128)(2,1)S(1)}, u32[]{:S(2)}, u32[]{:S(2)}) async-start(bf16[1,4,264,4,128]{4,3,2,0,1:T(4,128)(2,1)} %bitcast.70), calls=%async_computation.2 | async-start | bytes 2162688 | tf_op jit(solution)/shard_map/all_to_all | solution.py:142
  249.7 70.6 %reduce-scatter.4.cloned.1.call-start = ((), (), s32[]{:S(2)}) async-start(), calls=%async_computation.6 | async-start | bytes 737280
  287.6 3.2 collective-permute-start.20
  288.9 6.2 %collective-permute-start.21 = (bf16[1,1,256,128]{3,2,1,0:T(8,128)(2,1)S(1)}, bf16[1,1,256,128]{3,2,1,0:T(8,128)(2,1)S(1)}, u32[]{:S(2)}, u32[]{:S(2)}) collective-permute-start(bf16[1,1,256,128]{3,2,1,0:T(8,128)(2,1)S(1)} %get-tuple-element.124), channel_id=1, source_target_pairs={{2,0},{4,2},{6,4},{3,1},{5,3},{7,5},{10,8},{12,10},{14,12},{11,9},... | collective-permute-start | bytes 196616 | tf_op jit(solution)/shard_map/ppermute | solution.py:21
  298.6 23.6 %copy-start.7 = (bf16[1152,128]{1,0:T(8,128)(2,1)S(1)}, bf16[1152,128]{1,0:T(8,128)(2,1)}, u32[]{:S(2)}) copy-start(bf16[1152,128]{1,0:T(8,128)(2,1)} %param.22) | copy-start | bytes 884740
  298.6 78.1 %all-reduce.16.cloned.1.call-start = ((), (), s32[]{:S(2)}) async-start(), calls=%async_computation.5 | async-start | bytes 1179648 | tf_op jit(solution)/shard_map/psum | solution.py:194
  (4 other events, 8.9 us)
Sparse Core Ops, SparseCore 0:
  131.3 46.6 all-reduce.13
  298.7 21.4 reduce-scatter.3
  323.4 53.2 all-reduce.15
where the time goes:
time: 387 us; the launch traced here: 385 us
  waiting for transfers between devices  190 us (49%)
  starting transfers between devices  77.4 us (20%)
  local copies, waits for them, and re-layouts  69.9 us (18%)
  matrix products  18.6 us (5%)
  between operations  14.9 us (4%)
  other arithmetic  14.7 us (4%)
    psum x1, waiting for transfers between devices, body(): conv_grad = lax.psum(grad_share, ('phase', 'dp'))  53 us
    psum x1, waiting for transfers between devices, from_root(): return lax.psum(block, axis)  36.8 us
    ppermute x8, waiting for transfers between devices, extended(): lax.ppermute(head, axis, [((i + 1) % count, i) for i in range(ends)])  31.1 us
    ppermute x6, starting transfers between devices, passed_along(): return lax.ppermute(block, axis, route)  27.9 us
    scatter x1, local copies, waits for them, and re-layouts, body(): send_ctx = jnp.zeros((samples_dev, tile_count * capacity, BLK, channels),...  26.7 us
    ppermute x8, starting transfers between devices, extended(): lax.ppermute(tail, axis, [(i, (i + 1) % count) for i in range(ends)])  25.9 us
    all_to_all x1, waiting for transfers between devices, body(): lax.all_to_all(send_ctx, 'tile', split_axis=1, concat_axis=1, tiled=True)  24.5 us
    unnamed x4, waiting for transfers between devices  21.6 us
  transfers between devices with their start and end apart: 28, of which 25 were waited for; matrix products, arithmetic and copies ran while one was open for 19% of the time, Pallas kernels for 0%

commit v1 on v0

--- a/solution.py
+++ b/solution.py
@@ -6,6 +6,14 @@
 NSEG = 2
 BLK = 4
 BOUND = 8.0
+
+
+def clusters_supply(s0):
+    formed = lax.axis_size("tile")
+    n_now = jnp.split(s0, formed, axis=1)
+    earlier = jnp.stack(n_now)
+    now = lax.all_to_all(earlier, "tile", split_axis=0, concat_axis=0)
+    return jnp.concatenate(now, 1)
 
 
 def extended(cells, sides, width):
@@ -139,7 +147,7 @@
     send_weights = send_weights.reshape(samples_dev, tile_count, capacity, slot_total, BLK)
     send_cells = send_cells.reshape(samples_dev, tile_count, capacity, slot_total)
     got_ctx, got_weights, got_cells = (
-        lax.all_to_all(send_ctx, "tile", split_axis=1, concat_axis=1, tiled=True),
+        clusters_supply(send_ctx),
         lax.all_to_all(send_weights, "tile", split_axis=1, concat_axis=1, tiled=True),
         lax.all_to_all(send_cells, "tile", split_axis=1, concat_axis=1, tiled=True),
     )

time: 387 us -> 373 us (0.964)
  local copies, waits for them, and re-layouts: 69.9 us -> 51.4 us
  waiting for transfers between devices: 190 us -> 194 us
    scatter x1, local copies, waits for them, and re-layouts: 26.7 us -> 8.62 us  [body(): send_ctx = jnp.zeros((samples_dev, tile_count * capacity, BLK, channels),...]
    all_to_all x1, waiting for transfers between devices: 0.01 us -> 4.93 us  [body(): lax.all_to_all(send_weights, 'tile', split_axis=1, concat_axis=1, tiled=T...]
  transfers between devices with their start and end apart: 28 -> 28, of which waited for: 25 -> 26; matrix products, arithmetic and copies ran while one was open for 19% -> 15% of each run, Pallas kernels for 0% -> 0%
where the time goes in v1:
time: 373 us; the launch traced here: 371 us
  waiting for transfers between devices  194 us (52%)
  starting transfers between devices  75.8 us (20%)
  local copies, waits for them, and re-layouts  51.4 us (14%)
  matrix products  18.6 us (5%)
  other arithmetic  16.7 us (4%)
  between operations  15 us (4%)
    psum x1, waiting for transfers between devices, body(): conv_grad = lax.psum(grad_share, ('phase', 'dp'))  53 us
    psum x1, waiting for transfers between devices, from_root(): return lax.psum(block, axis)  36.8 us
    ppermute x8, waiting for transfers between devices, extended(): lax.ppermute(head, axis, [((i + 1) % count, i) for i in range(ends)])  31.1 us
    ppermute x6, starting transfers between devices, passed_along(): return lax.ppermute(block, axis, route)  27.9 us
    ppermute x8, starting transfers between devices, extended(): lax.ppermute(tail, axis, [(i, (i + 1) % count) for i in range(ends)])  25.9 us
    all_to_all x1, waiting for transfers between devices, clusters_supply(): now = lax.all_to_all(earlier, 'tile', split_axis=0, concat_axis=0)  23.8 us
    unnamed x4, waiting for transfers between devices  21.6 us
    ppermute x6, waiting for transfers between devices, passed_along(): return lax.ppermute(block, axis, route)  15.1 us
  transfers between devices with their start and end apart: 28, of which 26 were waited for; matrix products, arithmetic and copies ran while one was open for 15% of the time, Pallas kernels for 0%

profile of v1, /device:TPU:0, one launch (start us, length us, event | category | flops | bytes accessed | tf_op | source)
XLA Modules:
  0.0 371.3 jit_solution(10078268077607058202)
XLA Ops:
  8.2 4.9 %collective-permute-start = (bf16[1,3,1,176,128]{4,3,1,2,0:T(8,128)(2,1)S(1)}, bf16[1,3,1,176,128]{4,3,1,2,0:T(8,128)(2,1)S(1)}, u32[]{:S(2)}, u32[]{:S(2)}) collective-permute-start(bf16[1,3,1,176,128]{4,3,1,2,0:T(8,128)(2,1)S(1)} %fusion.83), channel_id=1, source_target_pairs={{0,2},{2,4},{4,6},{1,3},{3,5},{5,7},{8,10},{10,12},{12,14},{9,11},... | collective-permute-start | bytes 405512 | tf_op jit(solution)/shard_map/ppermute | solution.py:27
  15.9 4.1 %collective-permute-done.1 = bf16[1,3,1,176,128]{4,3,1,2,0:T(8,128)(2,1)S(1)} collective-permute-done((bf16[1,3,1,176,128]{4,3,1,2,0:T(8,128)(2,1)S(1)}, bf16[1,3,1,176,128]{4,3,1,2,0:T(8,128)(2,1)S(1)}, u32[]{:S(2)}, u32[]{:S(2)}) %collective-permute-start.1) | collective-permute-done | bytes 135200 | tf_op jit(solution)/shard_map/ppermute | solution.py:29
  21.8 3.4 collective-permute-start.2
  27.8 3.5 collective-permute-start.3
  33.8 4.4 %collective-permute-done.4 = bf16[1,3,1,176,128]{4,3,1,2,0:T(8,128)(2,1)S(1)} collective-permute-done((bf16[1,3,1,176,128]{4,3,1,2,0:T(8,128)(2,1)S(1)}, bf16[1,3,1,176,128]{4,3,1,2,0:T(8,128)(2,1)S(1)}, u32[]{:S(2)}, u32[]{:S(2)}) %collective-permute-start.4) | collective-permute-done | bytes 135200 | tf_op jit(solution)/shard_map/ppermute | solution.py:29
  39.3 4.4 %collective-permute-start.5 = (bf16[1,3,1,176,128]{4,3,1,2,0:T(8,128)(2,1)S(1)}, bf16[1,3,1,176,128]{4,3,1,2,0:T(8,128)(2,1)S(1)}, u32[]{:S(2)}, u32[]{:S(2)}) collective-permute-start(bf16[1,3,1,176,128]{4,3,1,2,0:T(8,128)(2,1)S(1)} %add_convert_fusion.5), channel_id=1, source_target_pairs={{0,8},{8,16},{16,24},{1,9},{9,17},{17,25},{2,10},{10,18},{18,26},{... | collective-permute-start | bytes 405512 | tf_op jit(solution)/shard_map/ppermute | solution.py:39
  46.3 3.5 collective-permute-start.6
  52.3 4.4 %collective-permute-done.7 = bf16[1,3,1,176,128]{4,3,1,2,0:T(8,128)(2,1)S(1)} collective-permute-done((bf16[1,3,1,176,128]{4,3,1,2,0:T(8,128)(2,1)S(1)}, bf16[1,3,1,176,128]{4,3,1,2,0:T(8,128)(2,1)S(1)}, u32[]{:S(2)}, u32[]{:S(2)}) %collective-permute-start.7) | collective-permute-done | bytes 135200 | tf_op jit(solution)/shard_map/ppermute | solution.py:29
  57.8 4.4 %collective-permute-start.8 = (bf16[1,3,1,176,128]{4,3,1,2,0:T(8,128)(2,1)S(1)}, bf16[1,3,1,176,128]{4,3,1,2,0:T(8,128)(2,1)S(1)}, u32[]{:S(2)}, u32[]{:S(2)}) collective-permute-start(bf16[1,3,1,176,128]{4,3,1,2,0:T(8,128)(2,1)S(1)} %add_convert_fusion.4), channel_id=1, source_target_pairs={{0,8},{8,16},{16,24},{1,9},{9,17},{17,25},{2,10},{10,18},{18,26},{... | collective-permute-start | bytes 405512 | tf_op jit(solution)/shard_map/ppermute | solution.py:39
  62.2 2.5 collective-permute-done.8
  66.1 4.6 %collective-permute-start.9 = (bf16[1,3,1,176,128]{4,3,1,2,0:T(8,128)(2,1)S(1)}, bf16[1,3,1,176,128]{4,3,1,2,0:T(8,128)(2,1)S(1)}, u32[]{:S(2)}, u32[]{:S(2)}) collective-permute-start(bf16[1,3,1,176,128]{4,3,1,2,0:T(8,128)(2,1)S(1)} %fusion.57), channel_id=1, source_target_pairs={{0,2},{2,4},{4,6},{1,3},{3,5},{5,7},{8,10},{10,12},{12,14},{9,11},... | collective-permute-start | bytes 405512 | tf_op jit(solution)/shard_map/ppermute | solution.py:27
  74.4 5.2 %collective-permute-start.11 = (bf16[1,3,1,176,128]{4,3,1,2,0:T(8,128)(2,1)S(1)}, bf16[1,3,1,176,128]{4,3,1,2,0:T(8,128)(2,1)S(1)}, u32[]{:S(2)}, u32[]{:S(2)}) collective-permute-start(bf16[1,3,1,176,128]{4,3,1,2,0:T(8,128)(2,1)S(1)} %get-tuple-element.92), channel_id=1, source_target_pairs={{0,8},{8,16},{16,24},{1,9},{9,17},{17,25},{2,10},{10,18},{18,26},{... | collective-permute-start | bytes 405512 | tf_op jit(solution)/shard_map/ppermute | solution.py:39
  79.6 2.5 collective-permute-done.11
  82.1 4.4 %collective-permute-start.12 = (bf16[1,3,1,176,128]{4,3,1,2,0:T(8,128)(2,1)S(1)}, bf16[1,3,1,176,128]{4,3,1,2,0:T(8,128)(2,1)S(1)}, u32[]{:S(2)}, u32[]{:S(2)}) collective-permute-start(bf16[1,3,1,176,128]{4,3,1,2,0:T(8,128)(2,1)S(1)} %collective-permute-done.11), channel_id=1, source_target_pairs={{0,2},{2,4},{4,6},{1,3},{3,5},{5,7},{8,10},{10,12},{12,14},{9,11},... | collective-permute-start | bytes 405512 | tf_op jit(solution)/shard_map/ppermute | solution.py:27
  89.0 4.4 %collective-permute-done.13 = bf16[1,3,1,176,128]{4,3,1,2,0:T(8,128)(2,1)S(1)} collective-permute-done((bf16[1,3,1,176,128]{4,3,1,2,0:T(8,128)(2,1)S(1)}, bf16[1,3,1,176,128]{4,3,1,2,0:T(8,128)(2,1)S(1)}, u32[]{:S(2)}, u32[]{:S(2)}) %collective-permute-start.13) | collective-permute-done | bytes 135200 | tf_op jit(solution)/shard_map/ppermute | solution.py:29
  94.6 5.3 %collective-permute-start.14 = (bf16[1,3,1,176,128]{4,3,1,2,0:T(8,128)(2,1)S(1)}, bf16[1,3,1,176,128]{4,3,1,2,0:T(8,128)(2,1)S(1)}, u32[]{:S(2)}, u32[]{:S(2)}) collective-permute-start(bf16[1,3,1,176,128]{4,3,1,2,0:T(8,128)(2,1)S(1)} %get-tuple-element.90), channel_id=1, source_target_pairs={{0,8},{8,16},{16,24},{1,9},{9,17},{17,25},{2,10},{10,18},{18,26},{... | collective-permute-start | bytes 405512 | tf_op jit(solution)/shard_map/ppermute | solution.py:39
  107.1 4.1 %collective-permute-done.16 = bf16[1,3,1,176,128]{4,3,1,2,0:T(8,128)(2,1)S(1)} collective-permute-done((bf16[1,3,1,176,128]{4,3,1,2,0:T(8,128)(2,1)S(1)}, bf16[1,3,1,176,128]{4,3,1,2,0:T(8,128)(2,1)S(1)}, u32[]{:S(2)}, u32[]{:S(2)}) %collective-permute-start.16) | collective-permute-done | bytes 135200 | tf_op jit(solution)/shard_map/ppermute | solution.py:29
  112.4 5.3 %collective-permute-start.17 = (bf16[1,3,1,176,128]{4,3,1,2,0:T(8,128)(2,1)S(1)}, bf16[1,3,1,176,128]{4,3,1,2,0:T(8,128)(2,1)S(1)}, u32[]{:S(2)}, u32[]{:S(2)}) collective-permute-start(bf16[1,3,1,176,128]{4,3,1,2,0:T(8,128)(2,1)S(1)} %get-tuple-element.88), channel_id=1, source_target_pairs={{0,8},{8,16},{16,24},{1,9},{9,17},{17,25},{2,10},{10,18},{18,26},{... | collective-permute-start | bytes 405512 | tf_op jit(solution)/shard_map/ppermute | solution.py:39
  124.7 4.4 %collective-permute-done.19 = bf16[1,3,1,176,128]{4,3,1,2,0:T(8,128)(2,1)S(1)} collective-permute-done((bf16[1,3,1,176,128]{4,3,1,2,0:T(8,128)(2,1)S(1)}, bf16[1,3,1,176,128]{4,3,1,2,0:T(8,128)(2,1)S(1)}, u32[]{:S(2)}, u32[]{:S(2)}) %collective-permute-start.19) | collective-permute-done | bytes 135200 | tf_op jit(solution)/shard_map/ppermute | solution.py:29
  133.5 3.5 all-to-all-start
  141.2 36.8 %all-reduce.14.cloned.1.call-done = bf16[4,1,3,1,176,128]{5,4,2,3,1,0:T(8,128)(2,1)} async-done(((bf16[4,1,3,1,176,128]{5,4,2,3,1,0:T(8,128)(2,1)}), bf16[4,1,3,1,176,128]{5,4,2,3,1,0:T(8,128)(2,1)}) %all-reduce.14.cloned.1.call-update) | async-done | bytes 540688 | tf_op jit(solution)/shard_map/psum | solution.py:44
  180.1 7.7 %fusion.26 = (bf16[132,2,4]{2,1,0:T(2,128)(2,1)S(1)}, bf16[132,2,4]{2,1,0:T(2,128)(2,1)S(1)}, bf16[132,2,4]{2,1,0:T(2,128)(2,1)S(1)}, bf16[132,2,4]{2,1,0:T(2,12...) fusion(pred[1,132,2,4,59]{4,3,2,1,0:T(4,128)(4,1)S(1)} %eq.411,, ...), kind=kLoop, calls=%fused_computation.55 | loop fusion | flops 1976832 | bytes 1279872 | tf_op jit(solution)/shard_map/reduce_sum | solution.py:111
  202.1 8.6 %scatter_fusion = bf16[1056,16,4]{1,2,0:T(4,128)(2,1)S(1)} fusion(bf16[1056,16,4]{1,2,0:T(4,128)(2,1)S(1)} %broadcast.618, s32[264]{0:T(512)S(1)} %fusion.62, bf16[264,16,4]{1,2,0:T(4,128)(2,1)S(1)} %copy.76), kind=kCustom, calls=%fused_computation.1 | custom fusion | bytes 102432 | tf_op jit(solution)/shard_map/scatter | solution.py:139
  212.4 8.6 %scatter_fusion.1 = bf16[1056,4,128]{2,1,0:T(4,128)(2,1)S(1)} fusion(bf16[1056,4,128]{2,1,0:T(4,128)(2,1)S(1)} %broadcast.620, s32[264]{0:T(512)S(1)} %fusion.62, bf16[264,4,128]{2,1,0:T(4,128)(2,1)S(1)} %bitcast.281), kind=kCustom, calls=%fused_computation.2 | custom fusion | bytes 812064 | tf_op jit(solution)/shard_map/scatter | solution.py:134
  221.1 4.6 %all-to-all-start.1 = ((bf16[1,4,264,16,4]{2,3,4,0,1:T(8,128)(2,1)}), bf16[1,4,264,16,4]{2,3,4,0,1:T(8,128)(2,1)S(1)}, u32[]{:S(2)}, u32[]{:S(2)}) async-start(bf16[1,4,264,16,4]{2,3,4,0,1:T(8,128)(2,1)} %copy.77), calls=%async_computation.1 | async-start | bytes 393216 | tf_op jit(solution)/shard_map/all_to_all | solution.py:151
  228.0 4.9 %all-to-all-done.1 = bf16[1,4,264,16,4]{2,3,4,0,1:T(8,128)(2,1)S(1)} async-done(((bf16[1,4,264,16,4]{2,3,4,0,1:T(8,128)(2,1)}), bf16[1,4,264,16,4]{2,3,4,0,1:T(8,128)(2,1)S(1)}, u32[]{:S(2)}, u32[]{:S(2)}) %all-to-all-start.1) | async-done | bytes 135200 | tf_op jit(solution)/shard_map/all_to_all | solution.py:151
  233.0 3.5 all-to-all-start.2
  237.6 23.8 %all-to-all-done.2 = bf16[4,1,1,264,4,128]{5,4,3,2,1,0:T(4,128)(2,1)S(1)} async-done(((bf16[4,1,1,264,4,128]{5,4,3,2,1,0:T(4,128)(2,1)}), bf16[4,1,1,264,4,128]{5,4,3,2,1,0:T(4,128)(2,1)S(1)}, u32[]{:S(2)}, u32[]{:S(2)}) %all-to-all-start.2) | async-done | bytes 1081376 | tf_op jit(solution)/shard_map/all_to_all | solution.py:15
  263.2 10.5 %fusion.4 = bf16[1024,128]{1,0:T(8,128)(2,1)S(1)} fusion(bf16[16896,128]{1,0:T(8,128)(2,1)S(1)} %bitcast.256, s32[16896]{0:T(1024)S(1)} %eq.358), kind=kOutput, calls=%fused_computation.15 | convolution fusion | flops 4446617600 | bytes 4655104 | tf_op jit(solution)/shard_map/while/body/eval_jaxpr/sxr,src->sxc/dot_general | solution.py:169
  276.9 4.3 %collective-permute-done.21 = bf16[1,1,256,128]{3,2,1,0:T(8,128)(2,1)S(1)} collective-permute-done((bf16[1,1,256,128]{3,2,1,0:T(8,128)(2,1)S(1)}, bf16[1,1,256,128]{3,2,1,0:T(8,128)(2,1)S(1)}, u32[]{:S(2)}, u32[]{:S(2)}) %collective-permute-start.21) | collective-permute-done | bytes 65568 | tf_op jit(solution)/shard_map/ppermute | solution.py:29
  284.8 21.6 %reduce-scatter.4.cloned.1.call-done = f32[32,1152]{1,0:T(8,128)} async-done(((f32[128,1152]{1,0:T(8,128)}), f32[32,1152]{1,0:T(8,128)}) %reduce-scatter.4.cloned.1.call-update) | async-done | bytes 147472
  309.9 53.0 %all-reduce.16.cloned.1.call-done = f32[32,1152]{0,1:T(8,128)} async-done(((f32[32,1152]{0,1:T(8,128)}), f32[32,1152]{0,1:T(8,128)}) %all-reduce.16.cloned.1.call-update) | async-done | bytes 147472 | tf_op jit(solution)/shard_map/psum | solution.py:202
  (226 shorter events, 85.4 us)
Async XLA Ops:
  7.2 13.6 %copy-start = (bf16[1,1152,128]{2,1,0:T(8,128)(2,1)S(1)}, bf16[1,1152,128]{2,1,0:T(8,128)(2,1)}, u32[]{:S(2)}) copy-start(bf16[1,1152,128]{2,1,0:T(8,128)(2,1)} %param.17) | copy-start | bytes 884740
  7.2 170.8 %all-reduce.14.cloned.1.call-start = ((), (), s32[]{:S(2)}) async-start(), calls=%async_computation.4 | async-start | bytes 1081344 | tf_op jit(solution)/shard_map/psum | solution.py:44
  8.2 7.8 %collective-permute-start = (bf16[1,3,1,176,128]{4,3,1,2,0:T(8,128)(2,1)S(1)}, bf16[1,3,1,176,128]{4,3,1,2,0:T(8,128)(2,1)S(1)}, u32[]{:S(2)}, u32[]{:S(2)}) collective-permute-start(bf16[1,3,1,176,128]{4,3,1,2,0:T(8,128)(2,1)S(1)} %fusion.83), channel_id=1, source_target_pairs={{0,2},{2,4},{4,6},{1,3},{3,5},{5,7},{8,10},{10,12},{12,14},{9,11},... | collective-permute-start | bytes 405512 | tf_op jit(solution)/shard_map/ppermute | solution.py:27
  13.1 6.9 %collective-permute-start.1 = (bf16[1,3,1,176,128]{4,3,1,2,0:T(8,128)(2,1)S(1)}, bf16[1,3,1,176,128]{4,3,1,2,0:T(8,128)(2,1)S(1)}, u32[]{:S(2)}, u32[]{:S(2)}) collective-permute-start(bf16[1,3,1,176,128]{4,3,1,2,0:T(8,128)(2,1)S(1)} %fusion.83), channel_id=1, source_target_pairs={{2,0},{4,2},{6,4},{3,1},{5,3},{7,5},{10,8},{12,10},{14,12},{11,9},... | collective-permute-start | bytes 405512 | tf_op jit(solution)/shard_map/ppermute | solution.py:29
  21.8 5.9 %collective-permute-start.2 = (bf16[1,3,1,176,128]{4,3,1,2,0:T(8,128)(2,1)S(1)}, bf16[1,3,1,176,128]{4,3,1,2,0:T(8,128)(2,1)S(1)}, u32[]{:S(2)}, u32[]{:S(2)}) collective-permute-start(bf16[1,3,1,176,128]{4,3,1,2,0:T(8,128)(2,1)S(1)} %add_convert_fusion.6), channel_id=1, source_target_pairs={{0,8},{8,16},{16,24},{1,9},{9,17},{17,25},{2,10},{10,18},{18,26},{... | collective-permute-start | bytes 405512 | tf_op jit(solution)/shard_map/ppermute | solution.py:39
  27.8 6.0 %collective-permute-start.3 = (bf16[1,3,1,176,128]{4,3,1,2,0:T(8,128)(2,1)S(1)}, bf16[1,3,1,176,128]{4,3,1,2,0:T(8,128)(2,1)S(1)}, u32[]{:S(2)}, u32[]{:S(2)}) collective-permute-start(bf16[1,3,1,176,128]{4,3,1,2,0:T(8,128)(2,1)S(1)} %fusion.56), channel_id=1, source_target_pairs={{0,2},{2,4},{4,6},{1,3},{3,5},{5,7},{8,10},{10,12},{12,14},{9,11},... | collective-permute-start | bytes 405512 | tf_op jit(solution)/shard_map/ppermute | solution.py:27
  31.3 6.9 %collective-permute-start.4 = (bf16[1,3,1,176,128]{4,3,1,2,0:T(8,128)(2,1)S(1)}, bf16[1,3,1,176,128]{4,3,1,2,0:T(8,128)(2,1)S(1)}, u32[]{:S(2)}, u32[]{:S(2)}) collective-permute-start(bf16[1,3,1,176,128]{4,3,1,2,0:T(8,128)(2,1)S(1)} %fusion.56), channel_id=1, source_target_pairs={{2,0},{4,2},{6,4},{3,1},{5,3},{7,5},{10,8},{12,10},{14,12},{11,9},... | collective-permute-start | bytes 405512 | tf_op jit(solution)/shard_map/ppermute | solution.py:29
  39.3 6.9 %collective-permute-start.5 = (bf16[1,3,1,176,128]{4,3,1,2,0:T(8,128)(2,1)S(1)}, bf16[1,3,1,176,128]{4,3,1,2,0:T(8,128)(2,1)S(1)}, u32[]{:S(2)}, u32[]{:S(2)}) collective-permute-start(bf16[1,3,1,176,128]{4,3,1,2,0:T(8,128)(2,1)S(1)} %add_convert_fusion.5), channel_id=1, source_target_pairs={{0,8},{8,16},{16,24},{1,9},{9,17},{17,25},{2,10},{10,18},{18,26},{... | collective-permute-start | bytes 405512 | tf_op jit(solution)/shard_map/ppermute | solution.py:39
  46.3 6.0 %collective-permute-start.6 = (bf16[1,3,1,176,128]{4,3,1,2,0:T(8,128)(2,1)S(1)}, bf16[1,3,1,176,128]{4,3,1,2,0:T(8,128)(2,1)S(1)}, u32[]{:S(2)}, u32[]{:S(2)}) collective-permute-start(bf16[1,3,1,176,128]{4,3,1,2,0:T(8,128)(2,1)S(1)} %bitcast_select_fusion.16), channel_id=1, source_target_pairs={{0,2},{2,4},{4,6},{1,3},{3,5},{5,7},{8,10},{10,12},{12,14},{9,11},... | collective-permute-start | bytes 405512 | tf_op jit(solution)/shard_map/ppermute | solution.py:27
  49.8 6.9 %collective-permute-start.7 = (bf16[1,3,1,176,128]{4,3,1,2,0:T(8,128)(2,1)S(1)}, bf16[1,3,1,176,128]{4,3,1,2,0:T(8,128)(2,1)S(1)}, u32[]{:S(2)}, u32[]{:S(2)}) collective-permute-start(bf16[1,3,1,176,128]{4,3,1,2,0:T(8,128)(2,1)S(1)} %bitcast_select_fusion.16), channel_id=1, source_target_pairs={{2,0},{4,2},{6,4},{3,1},{5,3},{7,5},{10,8},{12,10},{14,12},{11,9},... | collective-permute-start | bytes 405512 | tf_op jit(solution)/shard_map/ppermute | solution.py:29
  57.8 6.9 %collective-permute-start.8 = (bf16[1,3,1,176,128]{4,3,1,2,0:T(8,128)(2,1)S(1)}, bf16[1,3,1,176,128]{4,3,1,2,0:T(8,128)(2,1)S(1)}, u32[]{:S(2)}, u32[]{:S(2)}) collective-permute-start(bf16[1,3,1,176,128]{4,3,1,2,0:T(8,128)(2,1)S(1)} %add_convert_fusion.4), channel_id=1, source_target_pairs={{0,8},{8,16},{16,24},{1,9},{9,17},{17,25},{2,10},{10,18},{18,26},{... | collective-permute-start | bytes 405512 | tf_op jit(solution)/shard_map/ppermute | solution.py:39
  64.8 6.9 %collective-permute-start.10 = (bf16[1,3,1,176,128]{4,3,1,2,0:T(8,128)(2,1)S(1)}, bf16[1,3,1,176,128]{4,3,1,2,0:T(8,128)(2,1)S(1)}, u32[]{:S(2)}, u32[]{:S(2)}) collective-permute-start(bf16[1,3,1,176,128]{4,3,1,2,0:T(8,128)(2,1)S(1)} %fusion.57), channel_id=1, source_target_pairs={{2,0},{4,2},{6,4},{3,1},{5,3},{7,5},{10,8},{12,10},{14,12},{11,9},... | collective-permute-start | bytes 405512 | tf_op jit(solution)/shard_map/ppermute | solution.py:29
  66.1 7.1 %collective-permute-start.9 = (bf16[1,3,1,176,128]{4,3,1,2,0:T(8,128)(2,1)S(1)}, bf16[1,3,1,176,128]{4,3,1,2,0:T(8,128)(2,1)S(1)}, u32[]{:S(2)}, u32[]{:S(2)}) collective-permute-start(bf16[1,3,1,176,128]{4,3,1,2,0:T(8,128)(2,1)S(1)} %fusion.57), channel_id=1, source_target_pairs={{0,2},{2,4},{4,6},{1,3},{3,5},{5,7},{8,10},{10,12},{12,14},{9,11},... | collective-permute-start | bytes 405512 | tf_op jit(solution)/shard_map/ppermute | solution.py:27
  74.4 7.7 %collective-permute-start.11 = (bf16[1,3,1,176,128]{4,3,1,2,0:T(8,128)(2,1)S(1)}, bf16[1,3,1,176,128]{4,3,1,2,0:T(8,128)(2,1)S(1)}, u32[]{:S(2)}, u32[]{:S(2)}) collective-permute-start(bf16[1,3,1,176,128]{4,3,1,2,0:T(8,128)(2,1)S(1)} %get-tuple-element.92), channel_id=1, source_target_pairs={{0,8},{8,16},{16,24},{1,9},{9,17},{17,25},{2,10},{10,18},{18,26},{... | collective-permute-start | bytes 405512 | tf_op jit(solution)/shard_map/ppermute | solution.py:39
  82.1 6.9 %collective-permute-start.12 = (bf16[1,3,1,176,128]{4,3,1,2,0:T(8,128)(2,1)S(1)}, bf16[1,3,1,176,128]{4,3,1,2,0:T(8,128)(2,1)S(1)}, u32[]{:S(2)}, u32[]{:S(2)}) collective-permute-start(bf16[1,3,1,176,128]{4,3,1,2,0:T(8,128)(2,1)S(1)} %collective-permute-done.11), channel_id=1, source_target_pairs={{0,2},{2,4},{4,6},{1,3},{3,5},{5,7},{8,10},{10,12},{12,14},{9,11},... | collective-permute-start | bytes 405512 | tf_op jit(solution)/shard_map/ppermute | solution.py:27
  86.5 6.9 %collective-permute-start.13 = (bf16[1,3,1,176,128]{4,3,1,2,0:T(8,128)(2,1)S(1)}, bf16[1,3,1,176,128]{4,3,1,2,0:T(8,128)(2,1)S(1)}, u32[]{:S(2)}, u32[]{:S(2)}) collective-permute-start(bf16[1,3,1,176,128]{4,3,1,2,0:T(8,128)(2,1)S(1)} %collective-permute-done.11), channel_id=1, source_target_pairs={{2,0},{4,2},{6,4},{3,1},{5,3},{7,5},{10,8},{12,10},{14,12},{11,9},... | collective-permute-start | bytes 405512 | tf_op jit(solution)/shard_map/ppermute | solution.py:29
  93.9 5.9 %copy-start.6 = (s32[1,1,264,1]{2,3,1,0:T(1,128)S(1)}, s32[1,1,264,1]{2,3,1,0:T(1,128)}, u32[]{:S(2)}) copy-start(s32[1,1,264,1]{2,3,1,0:T(1,128)} %param.19) | copy-start | bytes 3172
  94.6 7.8 %collective-permute-start.14 = (bf16[1,3,1,176,128]{4,3,1,2,0:T(8,128)(2,1)S(1)}, bf16[1,3,1,176,128]{4,3,1,2,0:T(8,128)(2,1)S(1)}, u32[]{:S(2)}, u32[]{:S(2)}) collective-permute-start(bf16[1,3,1,176,128]{4,3,1,2,0:T(8,128)(2,1)S(1)} %get-tuple-element.90), channel_id=1, source_target_pairs={{0,8},{8,16},{16,24},{1,9},{9,17},{17,25},{2,10},{10,18},{18,26},{... | collective-permute-start | bytes 405512 | tf_op jit(solution)/shard_map/ppermute | solution.py:39
  102.4 4.7 %collective-permute-start.15 = (bf16[1,3,1,176,128]{4,3,1,2,0:T(8,128)(2,1)S(1)}, bf16[1,3,1,176,128]{4,3,1,2,0:T(8,128)(2,1)S(1)}, u32[]{:S(2)}, u32[]{:S(2)}) collective-permute-start(bf16[1,3,1,176,128]{4,3,1,2,0:T(8,128)(2,1)S(1)} %collective-permute-done.14), channel_id=1, source_target_pairs={{0,2},{2,4},{4,6},{1,3},{3,5},{5,7},{8,10},{10,12},{12,14},{9,11},... | collective-permute-start | bytes 405512 | tf_op jit(solution)/shard_map/ppermute | solution.py:27
  104.3 6.9 %collective-permute-start.16 = (bf16[1,3,1,176,128]{4,3,1,2,0:T(8,128)(2,1)S(1)}, bf16[1,3,1,176,128]{4,3,1,2,0:T(8,128)(2,1)S(1)}, u32[]{:S(2)}, u32[]{:S(2)}) collective-permute-start(bf16[1,3,1,176,128]{4,3,1,2,0:T(8,128)(2,1)S(1)} %collective-permute-done.14), channel_id=1, source_target_pairs={{2,0},{4,2},{6,4},{3,1},{5,3},{7,5},{10,8},{12,10},{14,12},{11,9},... | collective-permute-start | bytes 405512 | tf_op jit(solution)/shard_map/ppermute | solution.py:29
  112.4 7.8 %collective-permute-start.17 = (bf16[1,3,1,176,128]{4,3,1,2,0:T(8,128)(2,1)S(1)}, bf16[1,3,1,176,128]{4,3,1,2,0:T(8,128)(2,1)S(1)}, u32[]{:S(2)}, u32[]{:S(2)}) collective-permute-start(bf16[1,3,1,176,128]{4,3,1,2,0:T(8,128)(2,1)S(1)} %get-tuple-element.88), channel_id=1, source_target_pairs={{0,8},{8,16},{16,24},{1,9},{9,17},{17,25},{2,10},{10,18},{18,26},{... | collective-permute-start | bytes 405512 | tf_op jit(solution)/shard_map/ppermute | solution.py:39
  120.2 4.4 %collective-permute-start.18 = (bf16[1,3,1,176,128]{4,3,1,2,0:T(8,128)(2,1)S(1)}, bf16[1,3,1,176,128]{4,3,1,2,0:T(8,128)(2,1)S(1)}, u32[]{:S(2)}, u32[]{:S(2)}) collective-permute-start(bf16[1,3,1,176,128]{4,3,1,2,0:T(8,128)(2,1)S(1)} %collective-permute-done.17), channel_id=1, source_target_pairs={{0,2},{2,4},{4,6},{1,3},{3,5},{5,7},{8,10},{10,12},{12,14},{9,11},... | collective-permute-start | bytes 405512 | tf_op jit(solution)/shard_map/ppermute | solution.py:27
  122.2 6.9 %collective-permute-start.19 = (bf16[1,3,1,176,128]{4,3,1,2,0:T(8,128)(2,1)S(1)}, bf16[1,3,1,176,128]{4,3,1,2,0:T(8,128)(2,1)S(1)}, u32[]{:S(2)}, u32[]{:S(2)}) collective-permute-start(bf16[1,3,1,176,128]{4,3,1,2,0:T(8,128)(2,1)S(1)} %collective-permute-done.17), channel_id=1, source_target_pairs={{2,0},{4,2},{6,4},{3,1},{5,3},{7,5},{10,8},{12,10},{14,12},{11,9},... | collective-permute-start | bytes 405512 | tf_op jit(solution)/shard_map/ppermute | solution.py:29
  133.5 87.5 %all-to-all-start = ((s32[1,4,264,16]{2,3,0,1:T(8,128)}), s32[1,4,264,16]{2,3,0,1:T(8,128)S(1)}, u32[]{:S(2)}, u32[]{:S(2)}) async-start(s32[1,4,264,16]{2,3,0,1:T(8,128)} %copy.54), calls=%async_computation | async-start | bytes 196608 | tf_op jit(solution)/shard_map/all_to_all | solution.py:152
  138.7 40.2 %copy-start.4 = (bf16[128,118]{0,1:T(8,128)(2,1)S(1)}, bf16[128,118]{0,1:T(8,128)(2,1)}, u32[]{:S(2)}) copy-start(bf16[128,118]{0,1:T(8,128)(2,1)} %param.18) | copy-start | bytes 90628
  221.1 11.9 %all-to-all-start.1 = ((bf16[1,4,264,16,4]{2,3,4,0,1:T(8,128)(2,1)}), bf16[1,4,264,16,4]{2,3,4,0,1:T(8,128)(2,1)S(1)}, u32[]{:S(2)}, u32[]{:S(2)}) async-start(bf16[1,4,264,16,4]{2,3,4,0,1:T(8,128)(2,1)} %copy.77), calls=%async_computation.1 | async-start | bytes 393216 | tf_op jit(solution)/shard_map/all_to_all | solution.py:151
  233.0 28.5 %all-to-all-start.2 = ((bf16[4,1,1,264,4,128]{5,4,3,2,1,0:T(4,128)(2,1)}), bf16[4,1,1,264,4,128]{5,4,3,2,1,0:T(4,128)(2,1)S(1)}, u32[]{:S(2)}, u32[]{:S(2)}) async-start(bf16[4,1,1,264,4,128]{5,4,3,2,1,0:T(4,128)(2,1)} %pad_maximum_fusion), calls=%async_computation.2 | async-start | bytes 2162688 | tf_op jit(solution)/shard_map/all_to_all | solution.py:15
  236.5 69.9 %reduce-scatter.4.cloned.1.call-start = ((), (), s32[]{:S(2)}) async-start(), calls=%async_computation.6 | async-start | bytes 737280
  273.7 3.2 collective-permute-start.20
  275.0 6.2 %collective-permute-start.21 = (bf16[1,1,256,128]{3,2,1,0:T(8,128)(2,1)S(1)}, bf16[1,1,256,128]{3,2,1,0:T(8,128)(2,1)S(1)}, u32[]{:S(2)}, u32[]{:S(2)}) collective-permute-start(bf16[1,1,256,128]{3,2,1,0:T(8,128)(2,1)S(1)} %get-tuple-element.128), channel_id=1, source_target_pairs={{2,0},{4,2},{6,4},{3,1},{5,3},{7,5},{10,8},{12,10},{14,12},{11,9},... | collective-permute-start | bytes 196616 | tf_op jit(solution)/shard_map/ppermute | solution.py:29
  284.8 23.6 %copy-start.7 = (bf16[1152,128]{1,0:T(8,128)(2,1)S(1)}, bf16[1152,128]{1,0:T(8,128)(2,1)}, u32[]{:S(2)}) copy-start(bf16[1152,128]{1,0:T(8,128)(2,1)} %param.22) | copy-start | bytes 884740
  284.8 78.1 %all-reduce.16.cloned.1.call-start = ((), (), s32[]{:S(2)}) async-start(), calls=%async_computation.5 | async-start | bytes 1179648 | tf_op jit(solution)/shard_map/psum | solution.py:202
  (4 other events, 8.9 us)
Sparse Core Ops, SparseCore 0:
  131.3 46.6 all-reduce.13
  284.9 21.4 reduce-scatter.3
  309.5 53.2 all-reduce.15
